TPU v7x, 256 devices: a whole 4x4x8 slice. The times are simulated.
256 devices in a mesh: row: 16 (over y, z_hi, core), col: 16 (over z_lo, x).
Axes of the slice: x: 4, y: 4, z: 8 (z_hi: 2, z_lo: 4; z = z_hi * 4 + z_lo), core: 2. Of those that a mesh axis runs over, the one named last changes fastest.
Arguments:
- amplitudes: float32 [16, 16, 768, 768], P('row', 'col'), may hold values from -0.6 to 0.6
- integrals: float32 [16, 16, 768, 768], P('row', 'col'), may hold values from -6 to 6
- factors: float32 [16, 2048, 768], P('col', 'row'), may hold values from -0.21 to 0.21
- occ_energy: float32 [16], replicated, may hold values from -2 to -0.5
- vir_energy: float32 [768], replicated, may hold values from 0.5 to 3
Outputs:
- new_amplitudes: float32 [16, 16, 768, 768], P('row', 'col')
All inputs are finite; a program needn't handle non-finite values.
Results may differ from a plain program's by a relative error of at most 0.00005.
Values sent between devices are 32-bit elements; how exact they have to be, the bound alone decides.
No kernel may reach another device: no remote copies, remote signals or barrier semaphores. Data moves between devices by JAX's collectives and lax.ppermute only.
A program may use at most 128 MiB of HBM per device.

v0:
```python
import jax
import jax.numpy as jnp
from jax import lax
from jax.sharding import PartitionSpec as P


def pair_swap(tiles_in):
    arrived = lax.all_to_all(
        lax.all_to_all(tiles_in, "row", split_axis=2, concat_axis=0, tiled=True),
        "col",
        split_axis=0,
        concat_axis=1,
        tiled=True,
    )
    arrived = lax.all_to_all(arrived, "row", split_axis=1, concat_axis=2, tiled=True)
    return jnp.transpose(arrived, (1, 0, 3, 2))


def shards(amplitudes, integrals, factors, occ_energy, vir_energy):
    exact = lax.Precision.HIGHEST
    occ_rows = amplitudes.shape[0]
    occ_cols = amplitudes.shape[1]
    full_factors = lax.all_gather(factors, "row", axis=1, tiled=True)
    swapped = pair_swap(amplitudes)
    combined = 2.0 * amplitudes - swapped
    summed = lax.psum(jnp.einsum("ijab,jpb->pia", combined, full_factors, precision=exact), "col")
    coupled = jnp.einsum("pia,jpb->ijab", summed, full_factors, precision=exact)
    mirrored = pair_swap(coupled)
    residual = integrals + coupled + mirrored
    row_index = lax.axis_index("row")
    col_index = lax.axis_index("col")
    occ_left = lax.dynamic_slice_in_dim(occ_energy, row_index * occ_rows, occ_rows)
    occ_right = lax.dynamic_slice_in_dim(occ_energy, col_index * occ_cols, occ_cols)
    denominator = (
        occ_left[:, None, None, None]
        + occ_right[None, :, None, None]
        - vir_energy[None, None, :, None]
        - vir_energy[None, None, None, :]
    )
    return residual / denominator


def solution(mesh):
    return jax.shard_map(
        shards,
        mesh=mesh,
        in_specs=(
            P("row", "col", None, None),
            P("row", "col", None, None),
            P("col", "row", None),
            P(),
            P(),
        ),
        out_specs=P("row", "col", None, None),
        check_vma=False,
    )
```

profile of v0, /device:TPU:32, one launch (start us, length us, event | category | flops | bytes accessed | tf_op | source)
XLA Modules:
  0.0 686.9 jit_solution(6449531118020536048)
XLA Ops:
  6.5 5.5 copy.15
  12.0 10.3 %all-to-all-start = ((f32[1,1,768,768]{3,1,0,2:T(1,128)}), f32[1,1,768,768]{3,1,0,2:T(1,128)S(1)}, u32[]{:S(2)}, u32[]{:S(2)}) async-start(f32[1,1,768,768]{3,1,0,2:T(1,128)} %copy.15), calls=%async_computation | async-start | bytes 4718592 | tf_op jit(solution)/shard_map/all_to_all | solution.py:9
  22.3 0.0 all-gather.2.cloned.1.call-start
  22.4 0.7 all-gather.2.cloned.1.call-update
  23.1 67.3 %all-to-all-done = f32[1,1,768,768]{3,1,0,2:T(1,128)S(1)} async-done(((f32[1,1,768,768]{3,1,0,2:T(1,128)}), f32[1,1,768,768]{3,1,0,2:T(1,128)S(1)}, u32[]{:S(2)}, u32[]{:S(2)}) %all-to-all-start) | async-done | bytes 2359328 | tf_op jit(solution)/shard_map/all_to_all | solution.py:9
  90.4 0.2 copy.16
  90.5 90.1 %all_to_all.72 = f32[16,1,48,768]{3,2,1,0:T(8,128)} all-to-all(f32[16,1,48,768]{3,2,1,0:T(8,128)S(1)} %copy.16), channel_id=1, replica_groups=mesh['row'=16,'col'=16] {'col'}, dimensions={0} | all-to-all | bytes 4718592 | tf_op jit(solution)/shard_map/all_to_all | solution.py:8
  180.6 0.0 copy-start
  180.6 7.0 %all-to-all-start.2 = ((f32[1,16,48,768]{3,2,0,1:T(8,128)}), f32[1,16,48,768]{3,2,0,1:T(8,128)}, u32[]{:S(2)}, u32[]{:S(2)}) async-start(f32[1,16,48,768]{3,2,0,1:T(8,128)} %bitcast.49), calls=%async_computation.2 | async-start | bytes 4718592 | tf_op jit(solution)/shard_map/all_to_all | solution.py:15
  187.6 0.0 all-reduce.2.cloned.1.call-start
  187.7 0.0 copy-done
  187.7 2.0 copy.14
  189.6 0.0 all-gather.2.cloned.1.call-done
  189.6 57.6 %all-to-all-done.2 = f32[1,16,48,768]{3,2,0,1:T(8,128)} async-done(((f32[1,16,48,768]{3,2,0,1:T(8,128)}), f32[1,16,48,768]{3,2,0,1:T(8,128)}, u32[]{:S(2)}, u32[]{:S(2)}) %all-to-all-start.2) | async-done | bytes 2359328 | tf_op jit(solution)/shard_map/all_to_all | solution.py:15
  247.3 34.6 %fusion.4 = f32[2048,768]{0,1:T(8,128)} fusion(f32[1,2048,768]{2,1,0:T(8,128)} %all-gather.2.cloned.1.call-done, f32[1,1,768,768]{2,3,0,1:T(8,128)} %bitcast.5, f32[1,1,768,768]{2,3,0,1:T(8,128)} %copy.14), kind=kOutput, calls=%fused_computation.4 | convolution fusion | flops 14496694272 | bytes 17301504 | tf_op jit(solution)/shard_map/ijab,jpb->pia/dot_general | solution.py:26
  281.9 0.0 all-reduce.2.cloned.1.call-update
  281.9 178.8 %all-reduce.2.cloned.1.call-done = f32[2048,768]{0,1:T(8,128)} async-done(((f32[2048,768]{0,1:T(8,128)}), f32[2048,768]{0,1:T(8,128)}) %all-reduce.2.cloned.1.call-update) | async-done | bytes 6291472 | tf_op jit(solution)/shard_map/psum | solution.py:26
  460.8 18.7 %fusion.12 = f32[1,1,768,768]{3,2,0,1:T(8,128)S(1)} fusion(f32[2048,768]{0,1:T(8,128)} %all-reduce.2.cloned.1.call-done, f32[1,2048,768]{2,1,0:T(8,128)} %all-gather.2.cloned.1.call-done), kind=kOutput, calls=%fused_computation.12 | convolution fusion | flops 14495514624 | bytes 14942208 | tf_op jit(solution)/shard_map/pia,jpb->ijab/dot_general | solution.py:27
  479.4 0.0 copy-start.1
  479.5 2.4 copy.19
  481.9 0.0 copy-done.1
  481.9 67.1 %all_to_all.73 = f32[1,1,768,768]{3,0,1,2:T(1,128)S(1)} all-to-all(f32[1,1,768,768]{3,0,1,2:T(1,128)S(1)} %copy.19), channel_id=1, replica_groups=mesh['row'=16,'col'=16] {'row'}, dimensions={2} | all-to-all | bytes 4718592 | tf_op jit(solution)/shard_map/all_to_all | solution.py:9
  549.0 0.2 copy.20
  549.2 59.5 %all_to_all.74 = f32[16,1,48,768]{3,2,1,0:T(8,128)} all-to-all(f32[16,1,48,768]{3,2,1,0:T(8,128)S(1)} %copy.20), channel_id=1, replica_groups=mesh['row'=16,'col'=16] {'col'}, dimensions={0} | all-to-all | bytes 4718592 | tf_op jit(solution)/shard_map/all_to_all | solution.py:8
  608.7 0.0 copy-start.3
  608.7 0.0 copy-start.2
  608.7 4.8 all-to-all-start.5
  613.5 0.0 copy-done.3
  613.5 0.7 fusion.17
  615.4 0.0 copy-done.2
  615.5 57.7 %all-to-all-done.5 = f32[1,16,48,768]{3,2,0,1:T(8,128)S(1)} async-done(((f32[1,16,48,768]{3,2,0,1:T(8,128)}), f32[1,16,48,768]{3,2,0,1:T(8,128)S(1)}, u32[]{:S(2)}, u32[]{:S(2)}) %all-to-all-start.5) | async-done | bytes 2359328 | tf_op jit(solution)/shard_map/all_to_all | solution.py:15
  673.2 1.9 copy.22
  675.1 5.0 fusion.8
  (1 shorter events, 0.0 us)
Async XLA Ops:
  12.0 78.3 %all-to-all-start = ((f32[1,1,768,768]{3,1,0,2:T(1,128)}), f32[1,1,768,768]{3,1,0,2:T(1,128)S(1)}, u32[]{:S(2)}, u32[]{:S(2)}) async-start(f32[1,1,768,768]{3,1,0,2:T(1,128)} %copy.15), calls=%async_computation | async-start | bytes 4718592 | tf_op jit(solution)/shard_map/all_to_all | solution.py:9
  22.3 167.3 %all-gather.2.cloned.1.call-start = ((), (), s32[]{:S(2)}) async-start(), calls=%async_computation.6 | async-start | bytes 6684672 | tf_op jit(solution)/shard_map/all_gather | solution.py:23
  180.6 7.1 %copy-start = (f32[1,1,768,768]{3,2,1,0:T(8,128)S(1)}, f32[1,1,768,768]{3,2,1,0:T(8,128)}, u32[]{:S(2)}) copy-start(f32[1,1,768,768]{3,2,1,0:T(8,128)} %param.5) | copy-start | bytes 7077892
  180.6 66.7 %all-to-all-start.2 = ((f32[1,16,48,768]{3,2,0,1:T(8,128)}), f32[1,16,48,768]{3,2,0,1:T(8,128)}, u32[]{:S(2)}, u32[]{:S(2)}) async-start(f32[1,16,48,768]{3,2,0,1:T(8,128)} %bitcast.49), calls=%async_computation.2 | async-start | bytes 4718592 | tf_op jit(solution)/shard_map/all_to_all | solution.py:15
  187.6 273.1 %all-reduce.2.cloned.1.call-start = ((), (), s32[]{:S(2)}) async-start(), calls=%async_computation.7 | async-start | bytes 12582912 | tf_op jit(solution)/shard_map/psum | solution.py:26
  479.4 2.4 copy-start.1
  608.7 4.8 copy-start.3
  608.7 6.7 copy-start.2
  608.7 64.5 %all-to-all-start.5 = ((f32[1,16,48,768]{3,2,0,1:T(8,128)}), f32[1,16,48,768]{3,2,0,1:T(8,128)S(1)}, u32[]{:S(2)}, u32[]{:S(2)}) async-start(f32[1,16,48,768]{3,2,0,1:T(8,128)} %bitcast.47), calls=%async_computation.5 | async-start | bytes 4718592 | tf_op jit(solution)/shard_map/all_to_all | solution.py:15
Sparse Core Ops, SparseCore 0:
  25.9 141.4 all-gather.1
  282.1 178.6 all-reduce.1
where the time goes:
time: 687 us
  waiting for transfers between devices  362 us (53%)
  blocking collectives  217 us (32%)
  matrix products  53.3 us (8%)
  starting transfers between devices  22.2 us (3%)
  between operations  14.8 us (2%)
  local copies, waits for them, and re-layouts  12.8 us (2%)
    psum x1, waiting for transfers between devices, shards(): lax.psum(jnp.einsum('ijab,jpb->pia', combined, full_factors, precision=ex...  179 us
    all_to_all x2, blocking collectives, pair_swap(): lax.all_to_all(lax.all_to_all(tiles_in, 'row', split_axis=2, concat_axis=...  150 us
    all_to_all x2, waiting for transfers between devices, pair_swap(): lax.all_to_all(arrived, 'row', split_axis=1, concat_axis=2, tiled=True)  115 us
    all_to_all x1, waiting for transfers between devices, pair_swap(): lax.all_to_all(tiles_in, 'row', split_axis=2, concat_axis=0, tiled=True)  67.3 us
    all_to_all x1, blocking collectives, pair_swap(): lax.all_to_all(tiles_in, 'row', split_axis=2, concat_axis=0, tiled=True)  67.1 us
    dot_general x1, matrix products, shards(): jnp.einsum('ijab,jpb->pia', combined, full_factors, precision=exact)  34.6 us
    dot_general x1, matrix products, shards(): coupled = jnp.einsum('pia,jpb->ijab', summed, full_factors, precision=exact)  18.7 us
  transfers between devices with their start and end apart: 5, of which 4 were waited for; matrix products, arithmetic and copies ran while one was open for 0% of the time, Pallas kernels for 0%

commit v1 on v0

v1 whole, which is shorter than its diff:
```python
import jax
import jax.numpy as jnp
import numpy as np
from jax import lax
from jax.sharding import Mesh
from jax.sharding import PartitionSpec as P

AXES = ("y", "h", "k", "l", "x1", "x0")
SIZES = (4, 2, 2, 4, 2, 2)
ROW = ("y", "h", "k")
COL = ("l", "x1", "x0")


def send(value, to):
    pairs = []
    for source in range(256):
        y, h, k, l, x1, x0 = (int(v) for v in np.unravel_index(source, SIZES))
        y, h, k, l, x = to(y, h, k, l, 2 * x1 + x0)
        target = np.ravel_multi_index((y % 4, h % 2, k % 2, l % 4, (x % 4) >> 1, x % 2), SIZES)
        pairs.append((source, int(target)))
    return lax.ppermute(value, AXES, pairs)


def to_y(d):
    return lambda y, h, k, l, x: (y + d, h, k, l, x)


def to_x(d):
    return lambda y, h, k, l, x: (y, h, k, l, x + d)


def to_l(d):
    return lambda y, h, k, l, x: (y, h, k, l + d, x)


def to_z(d):
    return lambda y, h, k, l, x: (y, (4 * h + l + d) // 4, k, (l + d) % 4, x)


def to_h(y, h, k, l, x):
    return (y, h + 1, k, l, x)


def to_core(y, h, k, l, x):
    return (y, h, k + 1, l, x)


def to_mirror(y, h, k, l, x):
    return (l, x >> 1, x & 1, y, 2 * h + k)


def spread(d, e):
    return lambda y, h, k, l, x: (y + d, h, x & 1, l, 2 * ((x >> 1) ^ e) + k)


def collect(d, e):
    return lambda y, h, k, l, x: (y + d, h, k, l, x ^ (2 * e))


def pick(value, at):
    return lax.dynamic_index_in_dim(value, at, 0, keepdims=False)


def put(value, block, at):
    return lax.dynamic_update_index_in_dim(value, block, at, 0)


def swap_tile(tile):
    y, h, l, x1 = (lax.axis_index(n) for n in ("y", "h", "l", "x1"))
    z = 4 * h + l
    rows, columns = tile.shape
    parts = tile.reshape(8, rows // 8, columns)
    first = jnp.stack([
        send(pick(parts, 2 * ((y + d) % 4) + (x1 ^ e)), spread(d, e)) for e in range(2) for d in range(4)
    ])
    second = []
    for d in range(8):
        goal = (z + d) % 8
        piece = pick(first, 4 * ((goal >> 2) ^ x1) + (y - (goal & 3)) % 4)
        second.append(send(piece, to_z(d)) if d else piece)
    second = jnp.stack(second)
    out = jnp.zeros_like(parts)
    for e in range(2):
        for d in range(4):
            piece = pick(second, (z - (4 * (x1 ^ e) + (y + d) % 4)) % 8)
            if d or e:
                piece = send(piece, collect(d, e))
            out = put(out, piece, 2 * ((y - d) % 4) + (x1 ^ e))
    return out.reshape(rows, columns)


def reduce_rows(partial):
    y, h, k = (lax.axis_index(n) for n in ROW)
    n, columns = partial.shape
    b = n // 16
    q = partial.reshape(2, 8 * b, columns)
    q = pick(q, k) + send(pick(q, 1 - k), to_core)
    q = q.reshape(4, 2, b, columns)
    far = pick(q, (y + 2) % 4)
    up, down = send(far[0], to_y(1)), send(far[1], to_y(-1))
    after, before = pick(q, (y + 1) % 4), pick(q, (y + 3) % 4)
    after = jnp.stack([after[0] + up, after[1]])
    before = jnp.stack([before[0], before[1] + down])
    r = pick(q, y) + send(after, to_y(1)) + send(before, to_y(-1))
    return pick(r, h) + send(pick(r, 1 - h), to_h)


def gather_rows(block):
    y, h, k = (lax.axis_index(n) for n in ROW)
    b, columns = block.shape
    other = send(block, to_h)
    r = jnp.where(h == 0, jnp.stack([block, other]), jnp.stack([other, block]))
    f, g = send(r, to_y(1)), send(r, to_y(-1))
    e = jnp.stack([send(f[0], to_y(1)), send(g[1], to_y(-1))])
    q = jnp.zeros((4, 2, b, columns), block.dtype)
    for part, at in ((r, y), (f, (y + 3) % 4), (g, (y + 1) % 4), (e, (y + 2) % 4)):
        q = put(q, part, at)
    q = q.reshape(8 * b, columns)
    s = jnp.zeros((2, 8 * b, columns), block.dtype)
    s = put(put(s, q, k), send(q, to_core), 1 - k)
    return s.reshape(16 * b, columns)


def gather_cols(block):
    l, x1, x0 = (lax.axis_index(n) for n in COL)
    x = 2 * x1 + x0
    b, columns = block.shape
    s = jnp.zeros((16, b, columns), block.dtype)
    for d in range(4):
        own = send(block, to_l(d)) if d else block
        f, g = send(own, to_x(1)), send(own, to_x(-1))
        e = jnp.concatenate([send(f[: b // 2], to_x(1)), send(g[b // 2 :], to_x(-1))])
        for part, dx in ((own, 0), (f, 3), (g, 1), (e, 2)):
            from_x = (x + dx) % 4
            s = put(s, part, 8 * (from_x & 1) + 2 * ((l - d) % 4) + (from_x >> 1))
    return s.reshape(16 * b, columns)


def shards(amplitudes, integrals, factors, occ_energy, vir_energy):
    high = lax.Precision.HIGH
    tile, given, block = amplitudes[0, 0], integrals[0, 0], factors[0]
    row = 4 * lax.axis_index("y") + 2 * lax.axis_index("h") + lax.axis_index("k")
    col = 4 * lax.axis_index("l") + 2 * lax.axis_index("x1") + lax.axis_index("x0")

    row_factors = gather_cols(send(block, to_mirror))
    swapped = swap_tile(tile)
    col_factors = gather_rows(block)
    combined = 2.0 * swapped - tile.T
    partial = lax.dot_general(row_factors, combined, (((1,), (1,)), ((), ())), precision=high)
    summed = reduce_rows(partial)
    row_summed = gather_cols(send(summed, to_mirror))
    col_summed = gather_rows(summed)
    over_p = (((0,), (0,)), ((), ()))
    coupled = lax.dot_general(row_summed, col_factors, over_p, precision=high)
    mirrored = lax.dot_general(row_factors, col_summed, over_p, precision=high)
    denominator = occ_energy[row] + occ_energy[col] - vir_energy[:, None] - vir_energy[None, :]
    return ((given + coupled + mirrored) / denominator)[None, None]


def solution(mesh):
    fine = Mesh(mesh.devices.reshape(SIZES), AXES)
    return jax.shard_map(
        shards,
        mesh=fine,
        in_specs=(P(ROW, COL), P(ROW, COL), P(COL, ROW), P(), P()),
        out_specs=P(ROW, COL),
        check_vma=False,
    )
```

time: 687 us -> 549 us (0.80); the launches traced: 687 us -> 540 us
  blocking collectives: 217 us -> 0 us
  starting transfers between devices: 22.2 us -> 219 us
  waiting for transfers between devices: 362 us -> 252 us
  matrix products: 53.3 us -> 28.3 us
  local copies, waits for them, and re-layouts: 12.8 us -> 30.5 us
  between operations: 14.8 us -> 2.95 us
    ppermute x0 -> x80, waiting for transfers between devices: none -> 252 us  [send(): return lax.ppermute(value, AXES, pairs)]
    ppermute x0 -> x80, starting transfers between devices: none -> 219 us  [send(): return lax.ppermute(value, AXES, pairs)]
    all_to_all x3 -> x0, blocking collectives: 217 us -> none  [the longest x2 150 us: pair_swap(): lax.all_to_all(lax.all_to_all(tiles_in, 'row', split_axis=2, concat_axis=...]
    all_to_all x3 -> x0, waiting for transfers between devices: 183 us -> none  [the longest x2 115 us: pair_swap(): lax.all_to_all(arrived, 'row', split_axis=1, concat_axis=2, tiled=True)]
    psum x1 -> x0, waiting for transfers between devices: 179 us -> none  [shards(): lax.psum(jnp.einsum('ijab,jpb->pia', combined, full_factors, precision=ex...]
    dot_general x2 -> x3, matrix products: 53.3 us -> 28.3 us  [the longest x1 10.8 us: shards(): mirrored = lax.dot_general(row_factors, col_summed, over_p, precision=high)]
    all_to_all x3 -> x0, starting transfers between devices: 22.1 us -> none  [the longest x2 11.8 us: pair_swap(): lax.all_to_all(arrived, 'row', split_axis=1, concat_axis=2, tiled=True)]
    dynamic_update_slice x0 -> x39, local copies, waits for them, and re-layouts: none -> 9.12 us  [put(): return lax.dynamic_update_index_in_dim(value, block, at, 0)]
  transfers between devices with their start and end apart: 5 -> 80, of which waited for: 4 -> 36; matrix products, arithmetic and copies ran while one was open for 0% -> 7% of each run, Pallas kernels for 0% -> 0%
where the time goes in v1:
time: 549 us; the launch traced here: 540 us
  waiting for transfers between devices  252 us (46%)
  starting transfers between devices  219 us (40%)
  local copies, waits for them, and re-layouts  30.5 us (6%)
  matrix products  28.3 us (5%)
  other arithmetic  7.29 us (1%)
    ppermute x80, waiting for transfers between devices, send(): return lax.ppermute(value, AXES, pairs)  252 us
    ppermute x80, starting transfers between devices, send(): return lax.ppermute(value, AXES, pairs)  219 us
  transfers between devices with their start and end apart: 80, of which 36 were waited for; matrix products, arithmetic and copies ran while one was open for 7% of the time, Pallas kernels for 0%

profile of v1, /device:TPU:32, one launch (start us, length us, event | category | flops | bytes accessed | tf_op | source)
XLA Modules:
  0.0 540.2 jit_solution(2676224846370414849)
XLA Ops:
  0.0 2.7 dynamic-slice_bitcast_fusion.22
  5.1 3.0 collective-permute-start
  8.1 4.0 collective-permute-start.22
  14.1 6.5 %collective-permute-start.24 = (f32[96,768]{1,0:T(8,128)S(1)}, f32[96,768]{1,0:T(8,128)S(1)}, u32[]{:S(2)}, u32[]{:S(2)}) collective-permute-start(f32[96,768]{1,0:T(8,128)S(1)} %get-tuple-element.30), channel_id=1, source_target_pairs={{0,2},{1,18},{2,0},{3,16},{4,6},{5,22},{6,4},{7,20},{8,10},{9,26},... | collective-permute-start | bytes 884744 | tf_op jit(solution)/shard_map/ppermute | solution.py:21
  22.9 13.4 %collective-permute-start.26 = (f32[96,768]{1,0:T(8,128)S(1)}, f32[96,768]{1,0:T(8,128)S(1)}, u32[]{:S(2)}, u32[]{:S(2)}) collective-permute-start(f32[96,768]{1,0:T(8,128)S(1)} %get-tuple-element.28), channel_id=1, source_target_pairs={{0,130},{1,146},{2,128},{3,144},{4,134},{5,150},{6,132},{7,148},{8... | collective-permute-start | bytes 884744 | tf_op jit(solution)/shard_map/ppermute | solution.py:21
  36.6 5.7 %collective-permute-done.26 = f32[96,768]{1,0:T(8,128)S(1)} collective-permute-done((f32[96,768]{1,0:T(8,128)S(1)}, f32[96,768]{1,0:T(8,128)S(1)}, u32[]{:S(2)}, u32[]{:S(2)}) %collective-permute-start.26) | collective-permute-done | bytes 294944 | tf_op jit(solution)/shard_map/ppermute | solution.py:21
  42.3 6.3 %collective-permute-done.27 = f32[96,768]{1,0:T(8,128)S(1)} collective-permute-done((f32[96,768]{1,0:T(8,128)}, f32[96,768]{1,0:T(8,128)S(1)}, u32[]{:S(2)}, u32[]{:S(2)}) %collective-permute-start.27) | collective-permute-done | bytes 294944 | tf_op jit(solution)/shard_map/ppermute | solution.py:21
  50.1 4.3 collective-permute-start.28
  56.4 7.5 %collective-permute-start.29 = (f32[96,768]{1,0:T(8,128)}, f32[96,768]{1,0:T(8,128)S(1)}, u32[]{:S(2)}, u32[]{:S(2)}) collective-permute-start(f32[96,768]{1,0:T(8,128)} %get-tuple-element.24), channel_id=1, source_target_pairs={{0,8},{1,9},{2,10},{3,11},{4,12},{5,13},{6,14},{7,15},{8,32},{9,33... | collective-permute-start | bytes 884744 | tf_op jit(solution)/shard_map/ppermute | solution.py:21
  63.8 24.4 %collective-permute-start.30 = (f32[96,768]{1,0:T(8,128)}, f32[96,768]{1,0:T(8,128)S(1)}, u32[]{:S(2)}, u32[]{:S(2)}) collective-permute-start(f32[96,768]{1,0:T(8,128)} %get-tuple-element.23), channel_id=1, source_target_pairs={{0,12},{1,13},{2,14},{3,15},{4,32},{5,33},{6,34},{7,35},{8,36},{9,... | collective-permute-start | bytes 884744 | tf_op jit(solution)/shard_map/ppermute | solution.py:21
  88.3 5.1 collective-permute-start.32
  94.0 2.6 collective-permute-start.33
  97.7 3.3 collective-permute-start.34
  101.0 15.7 %collective-permute-done.30 = f32[96,768]{1,0:T(8,128)S(1)} collective-permute-done((f32[96,768]{1,0:T(8,128)}, f32[96,768]{1,0:T(8,128)S(1)}, u32[]{:S(2)}, u32[]{:S(2)}) %collective-permute-start.30) | collective-permute-done | bytes 294944 | tf_op jit(solution)/shard_map/ppermute | solution.py:21
  116.8 12.9 %collective-permute-start.1 = (f32[128,768]{1,0:T(8,128)S(1)}, f32[128,768]{1,0:T(8,128)S(1)}, u32[]{:S(2)}, u32[]{:S(2)}) collective-permute-start(f32[128,768]{1,0:T(8,128)S(1)} %collective-permute-done), channel_id=1, source_target_pairs={{0,1},{1,2},{2,3},{3,0},{4,5},{5,6},{6,7},{7,4},{8,9},{9,10},{10,1... | collective-permute-start | bytes 1179656 | tf_op jit(solution)/shard_map/ppermute | solution.py:21
  129.8 3.3 collective-permute-start.5
  133.2 7.0 %collective-permute-done.33 = f32[96,768]{1,0:T(8,128)S(1)} collective-permute-done((f32[96,768]{1,0:T(8,128)S(1)}, f32[96,768]{1,0:T(8,128)S(1)}, u32[]{:S(2)}, u32[]{:S(2)}) %collective-permute-start.33) | collective-permute-done | bytes 294944 | tf_op jit(solution)/shard_map/ppermute | solution.py:21
  140.3 5.7 %collective-permute-done.34 = f32[96,768]{1,0:T(8,128)S(1)} collective-permute-done((f32[96,768]{1,0:T(8,128)S(1)}, f32[96,768]{1,0:T(8,128)S(1)}, u32[]{:S(2)}, u32[]{:S(2)}) %collective-permute-start.34) | collective-permute-done | bytes 294944 | tf_op jit(solution)/shard_map/ppermute | solution.py:21
  148.8 8.8 %collective-permute-done.35 = f32[96,768]{1,0:T(8,128)S(1)} collective-permute-done((f32[96,768]{1,0:T(8,128)S(1)}, f32[96,768]{1,0:T(8,128)S(1)}, u32[]{:S(2)}, u32[]{:S(2)}) %collective-permute-start.35) | collective-permute-done | bytes 294944 | tf_op jit(solution)/shard_map/ppermute | solution.py:21
  160.0 5.5 %collective-permute-done.37 = f32[96,768]{1,0:T(8,128)S(1)} collective-permute-done((f32[96,768]{1,0:T(8,128)S(1)}, f32[96,768]{1,0:T(8,128)S(1)}, u32[]{:S(2)}, u32[]{:S(2)}) %collective-permute-start.37) | collective-permute-done | bytes 294944 | tf_op jit(solution)/shard_map/ppermute | solution.py:21
  165.6 7.2 %collective-permute-start.39 = (f32[96,768]{1,0:T(8,128)S(1)}, f32[96,768]{1,0:T(8,128)S(1)}, u32[]{:S(2)}, u32[]{:S(2)}) collective-permute-start(f32[96,768]{1,0:T(8,128)S(1)} %get-tuple-element.13), channel_id=1, source_target_pairs={{0,66},{1,67},{2,64},{3,65},{4,70},{5,71},{6,68},{7,69},{8,74},{9,... | collective-permute-start | bytes 884744 | tf_op jit(solution)/shard_map/ppermute | solution.py:21
  173.0 6.7 %collective-permute-done.39 = f32[96,768]{1,0:T(8,128)S(1)} collective-permute-done((f32[96,768]{1,0:T(8,128)S(1)}, f32[96,768]{1,0:T(8,128)S(1)}, u32[]{:S(2)}, u32[]{:S(2)}) %collective-permute-start.39) | collective-permute-done | bytes 294944 | tf_op jit(solution)/shard_map/ppermute | solution.py:21
  179.8 2.6 collective-permute-start.41
  182.4 10.2 %collective-permute-start.4 = (f32[64,768]{1,0:T(8,128)S(1)}, f32[64,768]{1,0:T(8,128)S(1)}, u32[]{:S(2)}, u32[]{:S(2)}) collective-permute-start(f32[64,768]{1,0:T(8,128)S(1)} %slice.117), channel_id=1, source_target_pairs={{0,3},{1,0},{2,1},{3,2},{4,7},{5,4},{6,5},{7,6},{8,11},{9,8},{10,9... | collective-permute-start | bytes 589832 | tf_op jit(solution)/shard_map/ppermute | solution.py:21
  194.5 2.7 collective-permute-start.3
  199.2 4.5 collective-permute-start.11
  203.9 3.7 collective-permute-done.3
  207.6 4.7 collective-permute-start.17
  212.6 3.4 collective-permute-done.6
  218.2 6.3 %collective-permute-done.11 = f32[128,768]{1,0:T(8,128)S(1)} collective-permute-done((f32[128,768]{1,0:T(8,128)S(1)}, f32[128,768]{1,0:T(8,128)S(1)}, u32[]{:S(2)}, u32[]{:S(2)}) %collective-permute-start.11) | collective-permute-done | bytes 393248 | tf_op jit(solution)/shard_map/ppermute | solution.py:21
  226.6 6.3 %collective-permute-done.16 = f32[128,768]{1,0:T(8,128)S(1)} collective-permute-done((f32[128,768]{1,0:T(8,128)S(1)}, f32[128,768]{1,0:T(8,128)S(1)}, u32[]{:S(2)}, u32[]{:S(2)}) %collective-permute-start.16) | collective-permute-done | bytes 393248 | tf_op jit(solution)/shard_map/ppermute | solution.py:21
  239.8 2.4 collective-permute-done.18
  242.2 8.3 %fusion.1 = f32[2,1024,768]{2,1,0:T(8,128)S(1)} fusion(f32[2,1024,768]{2,1,0:T(8,128)S(1)} %bitcast.284, f32[768,768]{1,0:T(8,128)S(1)} %bitcast.294, f32[1,1,768,768]{2,3,1,0:T(8,128)S(1)} %copy-done.4), kind=kOutput, calls=%fused_computation.6 | convolution fusion | flops 7248347136 | bytes 17301504 | tf_op jit(solution)/shard_map/dot_general | solution.py:149
  256.3 20.3 %collective-permute-done.68 = f32[128,768]{1,0:T(8,128)S(1)} collective-permute-done((f32[128,768]{1,0:T(8,128)S(1)}, f32[128,768]{1,0:T(8,128)S(1)}, u32[]{:S(2)}, u32[]{:S(2)}) %collective-permute-start.68) | collective-permute-done | bytes 393248 | tf_op jit(solution)/shard_map/ppermute | solution.py:21
  283.3 14.5 %collective-permute-done.70 = f32[2,128,768]{2,1,0:T(8,128)S(1)} collective-permute-done((f32[2,128,768]{2,1,0:T(8,128)}, f32[2,128,768]{2,1,0:T(8,128)S(1)}, u32[]{:S(2)}, u32[]{:S(2)}) %collective-permute-start.70) | collective-permute-done | bytes 786464 | tf_op jit(solution)/shard_map/ppermute | solution.py:21
  297.8 4.0 collective-permute-start.72
  306.0 3.6 collective-permute-done.72
  309.6 4.5 collective-permute-done.71
  317.7 3.2 collective-permute-start.45
  320.9 9.5 %collective-permute-done.43 = f32[128,768]{1,0:T(8,128)S(1)} collective-permute-done((f32[128,768]{1,0:T(8,128)S(1)}, f32[128,768]{1,0:T(8,128)S(1)}, u32[]{:S(2)}, u32[]{:S(2)}) %collective-permute-start.43) | collective-permute-done | bytes 393248 | tf_op jit(solution)/shard_map/ppermute | solution.py:21
  330.6 3.0 collective-permute-start.46
  333.7 16.2 %collective-permute-done.46 = f32[2,128,768]{2,1,0:T(8,128)S(1)} collective-permute-done((f32[2,128,768]{2,1,0:T(8,128)S(1)}, f32[2,128,768]{2,1,0:T(8,128)S(1)}, u32[]{:S(2)}, u32[]{:S(2)}) %collective-permute-start.46) | collective-permute-done | bytes 786464 | tf_op jit(solution)/shard_map/ppermute | solution.py:21
  350.0 3.5 collective-permute-done.44
  357.3 14.0 %collective-permute-done.47 = f32[128,768]{1,0:T(8,128)S(1)} collective-permute-done((f32[128,768]{1,0:T(8,128)S(1)}, f32[128,768]{1,0:T(8,128)S(1)}, u32[]{:S(2)}, u32[]{:S(2)}) %collective-permute-start.47) | collective-permute-done | bytes 393248 | tf_op jit(solution)/shard_map/ppermute | solution.py:21
  373.3 2.9 collective-permute-start.74
  381.0 31.0 %collective-permute-done.48 = f32[128,768]{1,0:T(8,128)S(1)} collective-permute-done((f32[128,768]{1,0:T(8,128)S(1)}, f32[128,768]{1,0:T(8,128)S(1)}, u32[]{:S(2)}, u32[]{:S(2)}) %collective-permute-start.48) | collective-permute-done | bytes 393248 | tf_op jit(solution)/shard_map/ppermute | solution.py:21
  412.0 7.6 %collective-permute-start.50 = (f32[128,768]{1,0:T(8,128)S(1)}, f32[128,768]{1,0:T(8,128)S(1)}, u32[]{:S(2)}, u32[]{:S(2)}) collective-permute-start(f32[128,768]{1,0:T(8,128)S(1)} %collective-permute-done.48), channel_id=1, source_target_pairs={{0,3},{1,0},{2,1},{3,2},{4,7},{5,4},{6,5},{7,6},{8,11},{9,8},{10,9... | collective-permute-start | bytes 1179656 | tf_op jit(solution)/shard_map/ppermute | solution.py:21
  419.8 3.2 collective-permute-start.76
  423.0 11.3 %collective-permute-start.53 = (f32[128,768]{1,0:T(8,128)S(1)}, f32[128,768]{1,0:T(8,128)S(1)}, u32[]{:S(2)}, u32[]{:S(2)}) collective-permute-start(f32[128,768]{1,0:T(8,128)S(1)} %collective-permute-done.48), channel_id=1, source_target_pairs={{0,4},{1,5},{2,6},{3,7},{4,8},{5,9},{6,10},{7,11},{8,12},{9,13},{1... | collective-permute-start | bytes 1179656 | tf_op jit(solution)/shard_map/ppermute | solution.py:21
  443.6 5.0 collective-permute-done.76
  451.0 15.1 %collective-permute-done.58 = f32[128,768]{1,0:T(8,128)S(1)} collective-permute-done((f32[128,768]{1,0:T(8,128)S(1)}, f32[128,768]{1,0:T(8,128)S(1)}, u32[]{:S(2)}, u32[]{:S(2)}) %collective-permute-start.58) | collective-permute-done | bytes 393248 | tf_op jit(solution)/shard_map/ppermute | solution.py:21
  466.1 8.5 %collective-permute-start.55 = (f32[128,768]{1,0:T(8,128)S(1)}, f32[128,768]{1,0:T(8,128)S(1)}, u32[]{:S(2)}, u32[]{:S(2)}) collective-permute-start(f32[128,768]{1,0:T(8,128)S(1)} %collective-permute-done.53), channel_id=1, source_target_pairs={{0,3},{1,0},{2,1},{3,2},{4,7},{5,4},{6,5},{7,6},{8,11},{9,8},{10,9... | collective-permute-start | bytes 1179656 | tf_op jit(solution)/shard_map/ppermute | solution.py:21
  474.6 3.2 collective-permute-start.60
  477.9 3.2 collective-permute-start.65
  481.2 2.9 collective-permute-done.55
  484.2 8.3 %collective-permute-done.60 = f32[128,768]{1,0:T(8,128)S(1)} collective-permute-done((f32[128,768]{1,0:T(8,128)S(1)}, f32[128,768]{1,0:T(8,128)S(1)}, u32[]{:S(2)}, u32[]{:S(2)}) %collective-permute-start.60) | collective-permute-done | bytes 393248 | tf_op jit(solution)/shard_map/ppermute | solution.py:21
  492.5 3.7 collective-permute-start.57
  496.3 4.6 collective-permute-done.65
  500.9 3.7 collective-permute-start.62
  505.2 3.7 collective-permute-start.67
  509.6 2.8 collective-permute-done.61
  512.6 3.3 collective-permute-done.66
  516.0 9.2 %fusion.24 = f32[768,768]{1,0:T(8,128)S(1)} fusion(f32[2048,768]{1,0:T(8,128)S(1)} %bitcast.296, f32[2048,768]{1,0:T(8,128)S(1)} %bitcast.297), kind=kOutput, calls=%fused_computation.136 | convolution fusion | flops 7247757312 | bytes 14942208 | tf_op jit(solution)/shard_map/dot_general | solution.py:154
  529.0 10.8 %fusion.5 = f32[1,1,768,768]{3,2,1,0:T(8,128)} fusion(f32[768,768]{1,0:T(8,128)S(1)} %fusion.24, f32[1,1,768,768]{3,2,1,0:T(8,128)S(1)} %copy-done.13, f32[768]{0:T(1024)S(1)} %copy-done.11, f32[768]{0:T(1024)S(1)} %broadcast_subtract_fusion, f32[2048,768]{1,0:T(8,128)S(1)} %bitcast.287, f32[2048,768]{1,0:T(8,128)S(1)} %bitcast.295), kind=kOutput, calls=%fused_computation.10 | convolution fusion | flops 7250116608 | bytes 19666944 | tf_op jit(solution)/shard_map/dot_general | solution.py:155
  (248 shorter events, 79.7 us)
Async XLA Ops:
  3.4 17.2 %collective-permute-start.21 = (f32[96,768]{1,0:T(8,128)}, f32[96,768]{1,0:T(8,128)S(1)}, u32[]{:S(2)}, u32[]{:S(2)}) collective-permute-start(f32[96,768]{1,0:T(8,128)} %get-tuple-element.33), channel_id=1, source_target_pairs={{0,64},{1,80},{2,66},{3,82},{4,68},{5,84},{6,70},{7,86},{8,72},{9,... | collective-permute-start | bytes 884744 | tf_op jit(solution)/shard_map/ppermute | solution.py:21
  5.1 83.2 %collective-permute-start = (f32[128,768]{1,0:T(8,128)S(1)}, f32[128,768]{1,0:T(8,128)S(1)}, u32[]{:S(2)}, u32[]{:S(2)}) collective-permute-start(f32[128,768]{1,0:T(8,128)S(1)} %bitcast.300), channel_id=1, source_target_pairs={{0,0},{1,16},{2,32},{3,48},{4,64},{5,80},{6,96},{7,112},{8,128},{9... | collective-permute-start | bytes 1179656 | tf_op jit(solution)/shard_map/ppermute | solution.py:21
  8.1 14.8 %collective-permute-start.22 = (f32[96,768]{1,0:T(8,128)}, f32[96,768]{1,0:T(8,128)S(1)}, u32[]{:S(2)}, u32[]{:S(2)}) collective-permute-start(f32[96,768]{1,0:T(8,128)} %get-tuple-element.32), channel_id=1, source_target_pairs={{0,128},{1,144},{2,130},{3,146},{4,132},{5,148},{6,134},{7,150},{8... | collective-permute-start | bytes 884744 | tf_op jit(solution)/shard_map/ppermute | solution.py:21
  12.1 24.3 %collective-permute-start.23 = (f32[96,768]{1,0:T(8,128)}, f32[96,768]{1,0:T(8,128)S(1)}, u32[]{:S(2)}, u32[]{:S(2)}) collective-permute-start(f32[96,768]{1,0:T(8,128)} %get-tuple-element.31), channel_id=1, source_target_pairs={{0,192},{1,208},{2,194},{3,210},{4,196},{5,212},{6,198},{7,214},{8... | collective-permute-start | bytes 884744 | tf_op jit(solution)/shard_map/ppermute | solution.py:21
  14.1 22.4 %collective-permute-start.24 = (f32[96,768]{1,0:T(8,128)S(1)}, f32[96,768]{1,0:T(8,128)S(1)}, u32[]{:S(2)}, u32[]{:S(2)}) collective-permute-start(f32[96,768]{1,0:T(8,128)S(1)} %get-tuple-element.30), channel_id=1, source_target_pairs={{0,2},{1,18},{2,0},{3,16},{4,6},{5,22},{6,4},{7,20},{8,10},{9,26},... | collective-permute-start | bytes 884744 | tf_op jit(solution)/shard_map/ppermute | solution.py:21
  20.6 15.9 %collective-permute-start.25 = (f32[96,768]{1,0:T(8,128)S(1)}, f32[96,768]{1,0:T(8,128)S(1)}, u32[]{:S(2)}, u32[]{:S(2)}) collective-permute-start(f32[96,768]{1,0:T(8,128)S(1)} %get-tuple-element.29), channel_id=1, source_target_pairs={{0,66},{1,82},{2,64},{3,80},{4,70},{5,86},{6,68},{7,84},{8,74},{9,... | collective-permute-start | bytes 884744 | tf_op jit(solution)/shard_map/ppermute | solution.py:21
  22.9 19.4 %collective-permute-start.26 = (f32[96,768]{1,0:T(8,128)S(1)}, f32[96,768]{1,0:T(8,128)S(1)}, u32[]{:S(2)}, u32[]{:S(2)}) collective-permute-start(f32[96,768]{1,0:T(8,128)S(1)} %get-tuple-element.28), channel_id=1, source_target_pairs={{0,130},{1,146},{2,128},{3,144},{4,134},{5,150},{6,132},{7,148},{8... | collective-permute-start | bytes 884744 | tf_op jit(solution)/shard_map/ppermute | solution.py:21
  50.1 43.9 %collective-permute-start.28 = (f32[96,768]{1,0:T(8,128)}, f32[96,768]{1,0:T(8,128)}, u32[]{:S(2)}, u32[]{:S(2)}) collective-permute-start(f32[96,768]{1,0:T(8,128)} %get-tuple-element.25), channel_id=1, source_target_pairs={{0,4},{1,5},{2,6},{3,7},{4,8},{5,9},{6,10},{7,11},{8,12},{9,13},{1... | collective-permute-start | bytes 884744 | tf_op jit(solution)/shard_map/ppermute | solution.py:21
  56.4 41.3 %collective-permute-start.29 = (f32[96,768]{1,0:T(8,128)}, f32[96,768]{1,0:T(8,128)S(1)}, u32[]{:S(2)}, u32[]{:S(2)}) collective-permute-start(f32[96,768]{1,0:T(8,128)} %get-tuple-element.24), channel_id=1, source_target_pairs={{0,8},{1,9},{2,10},{3,11},{4,12},{5,13},{6,14},{7,15},{8,32},{9,33... | collective-permute-start | bytes 884744 | tf_op jit(solution)/shard_map/ppermute | solution.py:21
  63.8 52.9 %collective-permute-start.30 = (f32[96,768]{1,0:T(8,128)}, f32[96,768]{1,0:T(8,128)S(1)}, u32[]{:S(2)}, u32[]{:S(2)}) collective-permute-start(f32[96,768]{1,0:T(8,128)} %get-tuple-element.23), channel_id=1, source_target_pairs={{0,12},{1,13},{2,14},{3,15},{4,32},{5,33},{6,34},{7,35},{8,36},{9,... | collective-permute-start | bytes 884744 | tf_op jit(solution)/shard_map/ppermute | solution.py:21
  88.3 41.4 %collective-permute-start.31 = (f32[96,768]{1,0:T(8,128)}, f32[96,768]{1,0:T(8,128)S(1)}, u32[]{:S(2)}, u32[]{:S(2)}) collective-permute-start(f32[96,768]{1,0:T(8,128)} %get-tuple-element.22), channel_id=1, source_target_pairs={{0,32},{1,33},{2,34},{3,35},{4,36},{5,37},{6,38},{7,39},{8,40},{9,... | collective-permute-start | bytes 884744 | tf_op jit(solution)/shard_map/ppermute | solution.py:21
  88.3 41.5 %collective-permute-start.32 = (f32[96,768]{1,0:T(8,128)}, f32[96,768]{1,0:T(8,128)S(1)}, u32[]{:S(2)}, u32[]{:S(2)}) collective-permute-start(f32[96,768]{1,0:T(8,128)} %get-tuple-element.21), channel_id=1, source_target_pairs={{0,36},{1,37},{2,38},{3,39},{4,40},{5,41},{6,42},{7,43},{8,44},{9,... | collective-permute-start | bytes 884744 | tf_op jit(solution)/shard_map/ppermute | solution.py:21
  94.0 46.2 %collective-permute-start.33 = (f32[96,768]{1,0:T(8,128)S(1)}, f32[96,768]{1,0:T(8,128)S(1)}, u32[]{:S(2)}, u32[]{:S(2)}) collective-permute-start(f32[96,768]{1,0:T(8,128)S(1)} %copy-done.10), channel_id=1, source_target_pairs={{0,40},{1,41},{2,42},{3,43},{4,44},{5,45},{6,46},{7,47},{8,0},{9,1... | collective-permute-start | bytes 884744 | tf_op jit(solution)/shard_map/ppermute | solution.py:21
  97.7 48.2 %collective-permute-start.34 = (f32[96,768]{1,0:T(8,128)S(1)}, f32[96,768]{1,0:T(8,128)S(1)}, u32[]{:S(2)}, u32[]{:S(2)}) collective-permute-start(f32[96,768]{1,0:T(8,128)S(1)} %copy-done.9), channel_id=1, source_target_pairs={{0,44},{1,45},{2,46},{3,47},{4,0},{5,1},{6,2},{7,3},{8,4},{9,5},{1... | collective-permute-start | bytes 884744 | tf_op jit(solution)/shard_map/ppermute | solution.py:21
  116.8 29.6 %collective-permute-start.1 = (f32[128,768]{1,0:T(8,128)S(1)}, f32[128,768]{1,0:T(8,128)S(1)}, u32[]{:S(2)}, u32[]{:S(2)}) collective-permute-start(f32[128,768]{1,0:T(8,128)S(1)} %collective-permute-done), channel_id=1, source_target_pairs={{0,1},{1,2},{2,3},{3,0},{4,5},{5,6},{6,7},{7,4},{8,9},{9,10},{10,1... | collective-permute-start | bytes 1179656 | tf_op jit(solution)/shard_map/ppermute | solution.py:21
  129.7 16.9 %collective-permute-start.2 = (f32[128,768]{1,0:T(8,128)S(1)}, f32[128,768]{1,0:T(8,128)S(1)}, u32[]{:S(2)}, u32[]{:S(2)}) collective-permute-start(f32[128,768]{1,0:T(8,128)S(1)} %collective-permute-done), channel_id=1, source_target_pairs={{0,3},{1,0},{2,1},{3,2},{4,7},{5,4},{6,5},{7,6},{8,11},{9,8},{10,9... | collective-permute-start | bytes 1179656 | tf_op jit(solution)/shard_map/ppermute | solution.py:21
  129.8 52.6 %collective-permute-start.5 = (f32[128,768]{1,0:T(8,128)S(1)}, f32[128,768]{1,0:T(8,128)S(1)}, u32[]{:S(2)}, u32[]{:S(2)}) collective-permute-start(f32[128,768]{1,0:T(8,128)S(1)} %collective-permute-done), channel_id=1, source_target_pairs={{0,4},{1,5},{2,6},{3,7},{4,8},{5,9},{6,10},{7,11},{8,12},{9,13},{1... | collective-permute-start | bytes 1179656 | tf_op jit(solution)/shard_map/ppermute | solution.py:21
  140.2 57.0 %collective-permute-start.10 = (f32[128,768]{1,0:T(8,128)S(1)}, f32[128,768]{1,0:T(8,128)S(1)}, u32[]{:S(2)}, u32[]{:S(2)}) collective-permute-start(f32[128,768]{1,0:T(8,128)S(1)} %collective-permute-done), channel_id=1, source_target_pairs={{0,8},{1,9},{2,10},{3,11},{4,12},{5,13},{6,14},{7,15},{8,0},{9,1},... | collective-permute-start | bytes 1179656 | tf_op jit(solution)/shard_map/ppermute | solution.py:21
  145.9 53.2 %collective-permute-start.15 = (f32[128,768]{1,0:T(8,128)S(1)}, f32[128,768]{1,0:T(8,128)S(1)}, u32[]{:S(2)}, u32[]{:S(2)}) collective-permute-start(f32[128,768]{1,0:T(8,128)S(1)} %collective-permute-done), channel_id=1, source_target_pairs={{0,12},{1,13},{2,14},{3,15},{4,0},{5,1},{6,2},{7,3},{8,4},{9,5},{1... | collective-permute-start | bytes 1179656 | tf_op jit(solution)/shard_map/ppermute | solution.py:21
  157.6 15.2 %collective-permute-start.38 = (f32[96,768]{1,0:T(8,128)S(1)}, f32[96,768]{1,0:T(8,128)S(1)}, u32[]{:S(2)}, u32[]{:S(2)}) collective-permute-start(f32[96,768]{1,0:T(8,128)S(1)} %get-tuple-element.14), channel_id=1, source_target_pairs={{0,2},{1,3},{2,0},{3,1},{4,6},{5,7},{6,4},{7,5},{8,10},{9,11},{10,... | collective-permute-start | bytes 884744 | tf_op jit(solution)/shard_map/ppermute | solution.py:21
  165.6 14.2 %collective-permute-start.39 = (f32[96,768]{1,0:T(8,128)S(1)}, f32[96,768]{1,0:T(8,128)S(1)}, u32[]{:S(2)}, u32[]{:S(2)}) collective-permute-start(f32[96,768]{1,0:T(8,128)S(1)} %get-tuple-element.13), channel_id=1, source_target_pairs={{0,66},{1,67},{2,64},{3,65},{4,70},{5,71},{6,68},{7,69},{8,74},{9,... | collective-permute-start | bytes 884744 | tf_op jit(solution)/shard_map/ppermute | solution.py:21
  172.8 19.8 %collective-permute-start.40 = (f32[96,768]{1,0:T(8,128)S(1)}, f32[96,768]{1,0:T(8,128)S(1)}, u32[]{:S(2)}, u32[]{:S(2)}) collective-permute-start(f32[96,768]{1,0:T(8,128)S(1)} %get-tuple-element.12), channel_id=1, source_target_pairs={{0,130},{1,131},{2,128},{3,129},{4,134},{5,135},{6,132},{7,133},{8... | collective-permute-start | bytes 884744 | tf_op jit(solution)/shard_map/ppermute | solution.py:21
  179.8 14.8 %collective-permute-start.41 = (f32[96,768]{1,0:T(8,128)S(1)}, f32[96,768]{1,0:T(8,128)S(1)}, u32[]{:S(2)}, u32[]{:S(2)}) collective-permute-start(f32[96,768]{1,0:T(8,128)S(1)} %get-tuple-element.11), channel_id=1, source_target_pairs={{0,194},{1,195},{2,192},{3,193},{4,198},{5,199},{6,196},{7,197},{8... | collective-permute-start | bytes 884744 | tf_op jit(solution)/shard_map/ppermute | solution.py:21
  182.4 21.3 %collective-permute-start.4 = (f32[64,768]{1,0:T(8,128)S(1)}, f32[64,768]{1,0:T(8,128)S(1)}, u32[]{:S(2)}, u32[]{:S(2)}) collective-permute-start(f32[64,768]{1,0:T(8,128)S(1)} %slice.117), channel_id=1, source_target_pairs={{0,3},{1,0},{2,1},{3,2},{4,7},{5,4},{6,5},{7,6},{8,11},{9,8},{10,9... | collective-permute-start | bytes 589832 | tf_op jit(solution)/shard_map/ppermute | solution.py:21
  192.7 14.9 %collective-permute-start.7 = (f32[128,768]{1,0:T(8,128)S(1)}, f32[128,768]{1,0:T(8,128)S(1)}, u32[]{:S(2)}, u32[]{:S(2)}) collective-permute-start(f32[128,768]{1,0:T(8,128)S(1)} %collective-permute-done.5), channel_id=1, source_target_pairs={{0,3},{1,0},{2,1},{3,2},{4,7},{5,4},{6,5},{7,6},{8,11},{9,8},{10,9... | collective-permute-start | bytes 1179656 | tf_op jit(solution)/shard_map/ppermute | solution.py:21
  194.5 13.1 %collective-permute-start.3 = (f32[64,768]{1,0:T(8,128)S(1)}, f32[64,768]{1,0:T(8,128)S(1)}, u32[]{:S(2)}, u32[]{:S(2)}) collective-permute-start(f32[64,768]{1,0:T(8,128)S(1)} %slice.116), channel_id=1, source_target_pairs={{0,1},{1,2},{2,3},{3,0},{4,5},{5,6},{6,7},{7,4},{8,9},{9,10},{10,1... | collective-permute-start | bytes 589832 | tf_op jit(solution)/shard_map/ppermute | solution.py:21
  197.3 18.8 %collective-permute-start.6 = (f32[128,768]{1,0:T(8,128)S(1)}, f32[128,768]{1,0:T(8,128)S(1)}, u32[]{:S(2)}, u32[]{:S(2)}) collective-permute-start(f32[128,768]{1,0:T(8,128)S(1)} %collective-permute-done.5), channel_id=1, source_target_pairs={{0,1},{1,2},{2,3},{3,0},{4,5},{5,6},{6,7},{7,4},{8,9},{9,10},{10,1... | collective-permute-start | bytes 1179656 | tf_op jit(solution)/shard_map/ppermute | solution.py:21
  199.2 25.3 %collective-permute-start.11 = (f32[128,768]{1,0:T(8,128)S(1)}, f32[128,768]{1,0:T(8,128)S(1)}, u32[]{:S(2)}, u32[]{:S(2)}) collective-permute-start(f32[128,768]{1,0:T(8,128)S(1)} %collective-permute-done.10), channel_id=1, source_target_pairs={{0,1},{1,2},{2,3},{3,0},{4,5},{5,6},{6,7},{7,4},{8,9},{9,10},{10,1... | collective-permute-start | bytes 1179656 | tf_op jit(solution)/shard_map/ppermute | solution.py:21
  203.7 14.4 %collective-permute-start.12 = (f32[128,768]{1,0:T(8,128)S(1)}, f32[128,768]{1,0:T(8,128)S(1)}, u32[]{:S(2)}, u32[]{:S(2)}) collective-permute-start(f32[128,768]{1,0:T(8,128)S(1)} %collective-permute-done.10), channel_id=1, source_target_pairs={{0,3},{1,0},{2,1},{3,2},{4,7},{5,4},{6,5},{7,6},{8,11},{9,8},{10,9... | collective-permute-start | bytes 1179656 | tf_op jit(solution)/shard_map/ppermute | solution.py:21
  207.6 25.3 %collective-permute-start.16 = (f32[128,768]{1,0:T(8,128)S(1)}, f32[128,768]{1,0:T(8,128)S(1)}, u32[]{:S(2)}, u32[]{:S(2)}) collective-permute-start(f32[128,768]{1,0:T(8,128)S(1)} %collective-permute-done.15), channel_id=1, source_target_pairs={{0,1},{1,2},{2,3},{3,0},{4,5},{5,6},{6,7},{7,4},{8,9},{9,10},{10,1... | collective-permute-start | bytes 1179656 | tf_op jit(solution)/shard_map/ppermute | solution.py:21
  207.6 18.9 %collective-permute-start.17 = (f32[128,768]{1,0:T(8,128)S(1)}, f32[128,768]{1,0:T(8,128)S(1)}, u32[]{:S(2)}, u32[]{:S(2)}) collective-permute-start(f32[128,768]{1,0:T(8,128)S(1)} %collective-permute-done.15), channel_id=1, source_target_pairs={{0,3},{1,0},{2,1},{3,2},{4,7},{5,4},{6,5},{7,6},{8,11},{9,8},{10,9... | collective-permute-start | bytes 1179656 | tf_op jit(solution)/shard_map/ppermute | solution.py:21
  216.0 19.0 %collective-permute-start.9 = (f32[64,768]{1,0:T(8,128)S(1)}, f32[64,768]{1,0:T(8,128)S(1)}, u32[]{:S(2)}, u32[]{:S(2)}) collective-permute-start(f32[64,768]{1,0:T(8,128)S(1)} %slice.119), channel_id=1, source_target_pairs={{0,3},{1,0},{2,1},{3,2},{4,7},{5,4},{6,5},{7,6},{8,11},{9,8},{10,9... | collective-permute-start | bytes 589832 | tf_op jit(solution)/shard_map/ppermute | solution.py:21
  218.1 19.0 %collective-permute-start.8 = (f32[64,768]{1,0:T(8,128)S(1)}, f32[64,768]{1,0:T(8,128)S(1)}, u32[]{:S(2)}, u32[]{:S(2)}) collective-permute-start(f32[64,768]{1,0:T(8,128)S(1)} %slice.118), channel_id=1, source_target_pairs={{0,1},{1,2},{2,3},{3,0},{4,5},{5,6},{6,7},{7,4},{8,9},{9,10},{10,1... | collective-permute-start | bytes 589832 | tf_op jit(solution)/shard_map/ppermute | solution.py:21
  224.5 12.8 %collective-permute-start.14 = (f32[64,768]{1,0:T(8,128)S(1)}, f32[64,768]{1,0:T(8,128)S(1)}, u32[]{:S(2)}, u32[]{:S(2)}) collective-permute-start(f32[64,768]{1,0:T(8,128)S(1)} %slice.121), channel_id=1, source_target_pairs={{0,3},{1,0},{2,1},{3,2},{4,7},{5,4},{6,5},{7,6},{8,11},{9,8},{10,9... | collective-permute-start | bytes 589832 | tf_op jit(solution)/shard_map/ppermute | solution.py:21
  226.5 13.1 %collective-permute-start.13 = (f32[64,768]{1,0:T(8,128)S(1)}, f32[64,768]{1,0:T(8,128)S(1)}, u32[]{:S(2)}, u32[]{:S(2)}) collective-permute-start(f32[64,768]{1,0:T(8,128)S(1)} %slice.120), channel_id=1, source_target_pairs={{0,1},{1,2},{2,3},{3,0},{4,5},{5,6},{6,7},{7,4},{8,9},{9,10},{10,1... | collective-permute-start | bytes 589832 | tf_op jit(solution)/shard_map/ppermute | solution.py:21
  254.1 61.0 %collective-permute-start.42 = (f32[1024,768]{1,0:T(8,128)}, f32[1024,768]{1,0:T(8,128)}, u32[]{:S(2)}, u32[]{:S(2)}) collective-permute-start(f32[1024,768]{1,0:T(8,128)} %dynamic-slice_bitcast_fusion), channel_id=1, source_target_pairs={{0,16},{1,17},{2,18},{3,19},{4,20},{5,21},{6,22},{7,23},{8,24},{9,... | collective-permute-start | bytes 9437192 | tf_op jit(solution)/shard_map/ppermute | solution.py:21
  254.1 22.4 %collective-permute-start.68 = (f32[128,768]{1,0:T(8,128)S(1)}, f32[128,768]{1,0:T(8,128)S(1)}, u32[]{:S(2)}, u32[]{:S(2)}) collective-permute-start(f32[128,768]{1,0:T(8,128)S(1)} %bitcast.301), channel_id=1, source_target_pairs={{0,32},{1,33},{2,34},{3,35},{4,36},{5,37},{6,38},{7,39},{8,40},{9,... | collective-permute-start | bytes 1179656 | tf_op jit(solution)/shard_map/ppermute | solution.py:21
  278.2 19.5 %collective-permute-start.70 = (f32[2,128,768]{2,1,0:T(8,128)}, f32[2,128,768]{2,1,0:T(8,128)S(1)}, u32[]{:S(2)}, u32[]{:S(2)}) collective-permute-start(f32[2,128,768]{2,1,0:T(8,128)} %maximum_select_fusion.1), channel_id=1, source_target_pairs={{0,192},{1,193},{2,194},{3,195},{4,196},{5,197},{6,198},{7,199},{8... | collective-permute-start | bytes 2359304 | tf_op jit(solution)/shard_map/ppermute | solution.py:21
  280.4 21.5 %collective-permute-start.69 = (f32[2,128,768]{2,1,0:T(8,128)}, f32[2,128,768]{2,1,0:T(8,128)}, u32[]{:S(2)}, u32[]{:S(2)}) collective-permute-start(f32[2,128,768]{2,1,0:T(8,128)} %maximum_select_fusion.1), channel_id=1, source_target_pairs={{0,64},{1,65},{2,66},{3,67},{4,68},{5,69},{6,70},{7,71},{8,72},{9,... | collective-permute-start | bytes 2359304 | tf_op jit(solution)/shard_map/ppermute | solution.py:21
  315.1 63.7 %collective-permute-start.73 = (f32[1024,768]{1,0:T(8,128)}, f32[1024,768]{1,0:T(8,128)}, u32[]{:S(2)}, u32[]{:S(2)}) collective-permute-start(f32[1024,768]{1,0:T(8,128)} %bitcast.110), channel_id=1, source_target_pairs={{0,16},{1,17},{2,18},{3,19},{4,20},{5,21},{6,22},{7,23},{8,24},{9,... | collective-permute-start | bytes 9437192 | tf_op jit(solution)/shard_map/ppermute | solution.py:21
  317.6 12.8 %collective-permute-start.43 = (f32[128,768]{1,0:T(8,128)S(1)}, f32[128,768]{1,0:T(8,128)S(1)}, u32[]{:S(2)}, u32[]{:S(2)}) collective-permute-start(f32[128,768]{1,0:T(8,128)S(1)} %get-tuple-element.7), channel_id=1, source_target_pairs={{0,64},{1,65},{2,66},{3,67},{4,68},{5,69},{6,70},{7,71},{8,72},{9,... | collective-permute-start | bytes 1179656 | tf_op jit(solution)/shard_map/ppermute | solution.py:21
  317.7 12.7 %collective-permute-start.45 = (f32[128,768]{1,0:T(8,128)S(1)}, f32[128,768]{1,0:T(8,128)S(1)}, u32[]{:S(2)}, u32[]{:S(2)}) collective-permute-start(f32[128,768]{1,0:T(8,128)S(1)} %get-tuple-element.9), channel_id=1, source_target_pairs={{0,192},{1,193},{2,194},{3,195},{4,196},{5,197},{6,198},{7,199},{8... | collective-permute-start | bytes 1179656 | tf_op jit(solution)/shard_map/ppermute | solution.py:21
  330.6 19.4 %collective-permute-start.46 = (f32[2,128,768]{2,1,0:T(8,128)S(1)}, f32[2,128,768]{2,1,0:T(8,128)S(1)}, u32[]{:S(2)}, u32[]{:S(2)}) collective-permute-start(f32[2,128,768]{2,1,0:T(8,128)S(1)} %pad_maximum_fusion.1), channel_id=1, source_target_pairs={{0,192},{1,193},{2,194},{3,195},{4,196},{5,197},{6,198},{7,199},{8... | collective-permute-start | bytes 2359304 | tf_op jit(solution)/shard_map/ppermute | solution.py:21
  333.7 19.9 %collective-permute-start.44 = (f32[2,128,768]{2,1,0:T(8,128)S(1)}, f32[2,128,768]{2,1,0:T(8,128)S(1)}, u32[]{:S(2)}, u32[]{:S(2)}) collective-permute-start(f32[2,128,768]{2,1,0:T(8,128)S(1)} %pad_maximum_fusion), channel_id=1, source_target_pairs={{0,64},{1,65},{2,66},{3,67},{4,68},{5,69},{6,70},{7,71},{8,72},{9,... | collective-permute-start | bytes 2359304 | tf_op jit(solution)/shard_map/ppermute | solution.py:21
  354.8 16.5 %collective-permute-start.47 = (f32[128,768]{1,0:T(8,128)S(1)}, f32[128,768]{1,0:T(8,128)S(1)}, u32[]{:S(2)}, u32[]{:S(2)}) collective-permute-start(f32[128,768]{1,0:T(8,128)S(1)} %dynamic-slice_bitcast_fusion.7), channel_id=1, source_target_pairs={{0,32},{1,33},{2,34},{3,35},{4,36},{5,37},{6,38},{7,39},{8,40},{9,... | collective-permute-start | bytes 1179656 | tf_op jit(solution)/shard_map/ppermute | solution.py:21
  371.4 40.7 %collective-permute-start.48 = (f32[128,768]{1,0:T(8,128)S(1)}, f32[128,768]{1,0:T(8,128)S(1)}, u32[]{:S(2)}, u32[]{:S(2)}) collective-permute-start(f32[128,768]{1,0:T(8,128)S(1)} %bitcast_add_fusion.3), channel_id=1, source_target_pairs={{0,0},{1,16},{2,32},{3,48},{4,64},{5,80},{6,96},{7,112},{8,128},{9... | collective-permute-start | bytes 1179656 | tf_op jit(solution)/shard_map/ppermute | solution.py:21
  373.3 46.3 %collective-permute-start.74 = (f32[128,768]{1,0:T(8,128)S(1)}, f32[128,768]{1,0:T(8,128)S(1)}, u32[]{:S(2)}, u32[]{:S(2)}) collective-permute-start(f32[128,768]{1,0:T(8,128)S(1)} %bitcast_add_fusion.3), channel_id=1, source_target_pairs={{0,32},{1,33},{2,34},{3,35},{4,36},{5,37},{6,38},{7,39},{8,40},{9,... | collective-permute-start | bytes 1179656 | tf_op jit(solution)/shard_map/ppermute | solution.py:21
  412.0 23.4 %collective-permute-start.49 = (f32[128,768]{1,0:T(8,128)S(1)}, f32[128,768]{1,0:T(8,128)S(1)}, u32[]{:S(2)}, u32[]{:S(2)}) collective-permute-start(f32[128,768]{1,0:T(8,128)S(1)} %collective-permute-done.48), channel_id=1, source_target_pairs={{0,1},{1,2},{2,3},{3,0},{4,5},{5,6},{6,7},{7,4},{8,9},{9,10},{10,1... | collective-permute-start | bytes 1179656 | tf_op jit(solution)/shard_map/ppermute | solution.py:21
  412.0 23.3 %collective-permute-start.50 = (f32[128,768]{1,0:T(8,128)S(1)}, f32[128,768]{1,0:T(8,128)S(1)}, u32[]{:S(2)}, u32[]{:S(2)}) collective-permute-start(f32[128,768]{1,0:T(8,128)S(1)} %collective-permute-done.48), channel_id=1, source_target_pairs={{0,3},{1,0},{2,1},{3,2},{4,7},{5,4},{6,5},{7,6},{8,11},{9,8},{10,9... | collective-permute-start | bytes 1179656 | tf_op jit(solution)/shard_map/ppermute | solution.py:21
  419.7 29.3 %collective-permute-start.75 = (f32[2,128,768]{2,1,0:T(8,128)S(1)}, f32[2,128,768]{2,1,0:T(8,128)S(1)}, u32[]{:S(2)}, u32[]{:S(2)}) collective-permute-start(f32[2,128,768]{2,1,0:T(8,128)S(1)} %maximum_select_fusion.3), channel_id=1, source_target_pairs={{0,64},{1,65},{2,66},{3,67},{4,68},{5,69},{6,70},{7,71},{8,72},{9,... | collective-permute-start | bytes 2359304 | tf_op jit(solution)/shard_map/ppermute | solution.py:21
  419.8 28.8 %collective-permute-start.76 = (f32[2,128,768]{2,1,0:T(8,128)S(1)}, f32[2,128,768]{2,1,0:T(8,128)S(1)}, u32[]{:S(2)}, u32[]{:S(2)}) collective-permute-start(f32[2,128,768]{2,1,0:T(8,128)S(1)} %maximum_select_fusion.3), channel_id=1, source_target_pairs={{0,192},{1,193},{2,194},{3,195},{4,196},{5,197},{6,198},{7,199},{8... | collective-permute-start | bytes 2359304 | tf_op jit(solution)/shard_map/ppermute | solution.py:21
  423.0 16.6 %collective-permute-start.53 = (f32[128,768]{1,0:T(8,128)S(1)}, f32[128,768]{1,0:T(8,128)S(1)}, u32[]{:S(2)}, u32[]{:S(2)}) collective-permute-start(f32[128,768]{1,0:T(8,128)S(1)} %collective-permute-done.48), channel_id=1, source_target_pairs={{0,4},{1,5},{2,6},{3,7},{4,8},{5,9},{6,10},{7,11},{8,12},{9,13},{1... | collective-permute-start | bytes 1179656 | tf_op jit(solution)/shard_map/ppermute | solution.py:21
  439.6 26.4 %collective-permute-start.58 = (f32[128,768]{1,0:T(8,128)S(1)}, f32[128,768]{1,0:T(8,128)S(1)}, u32[]{:S(2)}, u32[]{:S(2)}) collective-permute-start(f32[128,768]{1,0:T(8,128)S(1)} %collective-permute-done.48), channel_id=1, source_target_pairs={{0,8},{1,9},{2,10},{3,11},{4,12},{5,13},{6,14},{7,15},{8,0},{9,1},... | collective-permute-start | bytes 1179656 | tf_op jit(solution)/shard_map/ppermute | solution.py:21
  441.6 33.0 %collective-permute-start.63 = (f32[128,768]{1,0:T(8,128)S(1)}, f32[128,768]{1,0:T(8,128)S(1)}, u32[]{:S(2)}, u32[]{:S(2)}) collective-permute-start(f32[128,768]{1,0:T(8,128)S(1)} %collective-permute-done.48), channel_id=1, source_target_pairs={{0,12},{1,13},{2,14},{3,15},{4,0},{5,1},{6,2},{7,3},{8,4},{9,5},{1... | collective-permute-start | bytes 1179656 | tf_op jit(solution)/shard_map/ppermute | solution.py:21
  443.6 31.0 %collective-permute-start.54 = (f32[128,768]{1,0:T(8,128)S(1)}, f32[128,768]{1,0:T(8,128)S(1)}, u32[]{:S(2)}, u32[]{:S(2)}) collective-permute-start(f32[128,768]{1,0:T(8,128)S(1)} %collective-permute-done.53), channel_id=1, source_target_pairs={{0,1},{1,2},{2,3},{3,0},{4,5},{5,6},{6,7},{7,4},{8,9},{9,10},{10,1... | collective-permute-start | bytes 1179656 | tf_op jit(solution)/shard_map/ppermute | solution.py:21
  448.7 29.2 %collective-permute-start.78 = (f32[128,768]{1,0:T(8,128)S(1)}, f32[128,768]{1,0:T(8,128)S(1)}, u32[]{:S(2)}, u32[]{:S(2)}) collective-permute-start(f32[128,768]{1,0:T(8,128)S(1)} %slice_bitcast_fusion), channel_id=1, source_target_pairs={{0,192},{1,193},{2,194},{3,195},{4,196},{5,197},{6,198},{7,199},{8... | collective-permute-start | bytes 1179656 | tf_op jit(solution)/shard_map/ppermute | solution.py:21
  449.0 28.8 %collective-permute-start.77 = (f32[128,768]{1,0:T(8,128)S(1)}, f32[128,768]{1,0:T(8,128)S(1)}, u32[]{:S(2)}, u32[]{:S(2)}) collective-permute-start(f32[128,768]{1,0:T(8,128)S(1)} %slice_bitcast_fusion.1), channel_id=1, source_target_pairs={{0,64},{1,65},{2,66},{3,67},{4,68},{5,69},{6,70},{7,71},{8,72},{9,... | collective-permute-start | bytes 1179656 | tf_op jit(solution)/shard_map/ppermute | solution.py:21
  466.1 18.0 %collective-permute-start.55 = (f32[128,768]{1,0:T(8,128)S(1)}, f32[128,768]{1,0:T(8,128)S(1)}, u32[]{:S(2)}, u32[]{:S(2)}) collective-permute-start(f32[128,768]{1,0:T(8,128)S(1)} %collective-permute-done.53), channel_id=1, source_target_pairs={{0,3},{1,0},{2,1},{3,2},{4,7},{5,4},{6,5},{7,6},{8,11},{9,8},{10,9... | collective-permute-start | bytes 1179656 | tf_op jit(solution)/shard_map/ppermute | solution.py:21
  474.6 21.6 %collective-permute-start.59 = (f32[128,768]{1,0:T(8,128)S(1)}, f32[128,768]{1,0:T(8,128)S(1)}, u32[]{:S(2)}, u32[]{:S(2)}) collective-permute-start(f32[128,768]{1,0:T(8,128)S(1)} %collective-permute-done.58), channel_id=1, source_target_pairs={{0,1},{1,2},{2,3},{3,0},{4,5},{5,6},{6,7},{7,4},{8,9},{9,10},{10,1... | collective-permute-start | bytes 1179656 | tf_op jit(solution)/shard_map/ppermute | solution.py:21
  474.6 17.9 %collective-permute-start.60 = (f32[128,768]{1,0:T(8,128)S(1)}, f32[128,768]{1,0:T(8,128)S(1)}, u32[]{:S(2)}, u32[]{:S(2)}) collective-permute-start(f32[128,768]{1,0:T(8,128)S(1)} %collective-permute-done.58), channel_id=1, source_target_pairs={{0,3},{1,0},{2,1},{3,2},{4,7},{5,4},{6,5},{7,6},{8,11},{9,8},{10,9... | collective-permute-start | bytes 1179656 | tf_op jit(solution)/shard_map/ppermute | solution.py:21
  477.8 26.8 %collective-permute-start.64 = (f32[128,768]{1,0:T(8,128)S(1)}, f32[128,768]{1,0:T(8,128)S(1)}, u32[]{:S(2)}, u32[]{:S(2)}) collective-permute-start(f32[128,768]{1,0:T(8,128)S(1)} %collective-permute-done.63), channel_id=1, source_target_pairs={{0,1},{1,2},{2,3},{3,0},{4,5},{5,6},{6,7},{7,4},{8,9},{9,10},{10,1... | collective-permute-start | bytes 1179656 | tf_op jit(solution)/shard_map/ppermute | solution.py:21
  477.9 23.1 %collective-permute-start.65 = (f32[128,768]{1,0:T(8,128)S(1)}, f32[128,768]{1,0:T(8,128)S(1)}, u32[]{:S(2)}, u32[]{:S(2)}) collective-permute-start(f32[128,768]{1,0:T(8,128)S(1)} %collective-permute-done.63), channel_id=1, source_target_pairs={{0,3},{1,0},{2,1},{3,2},{4,7},{5,4},{6,5},{7,6},{8,11},{9,8},{10,9... | collective-permute-start | bytes 1179656 | tf_op jit(solution)/shard_map/ppermute | solution.py:21
  484.1 41.9 %collective-permute-start.79 = (f32[1024,768]{1,0:T(8,128)S(1)}, f32[1024,768]{1,0:T(8,128)S(1)}, u32[]{:S(2)}, u32[]{:S(2)}) collective-permute-start(f32[1024,768]{1,0:T(8,128)S(1)} %bitcast.288), channel_id=1, source_target_pairs={{0,16},{1,17},{2,18},{3,19},{4,20},{5,21},{6,22},{7,23},{8,24},{9,... | collective-permute-start | bytes 9437192 | tf_op jit(solution)/shard_map/ppermute | solution.py:21
  492.5 12.6 %collective-permute-start.57 = (f32[64,768]{1,0:T(8,128)S(1)}, f32[64,768]{1,0:T(8,128)S(1)}, u32[]{:S(2)}, u32[]{:S(2)}) collective-permute-start(f32[64,768]{1,0:T(8,128)S(1)} %slice.127), channel_id=1, source_target_pairs={{0,3},{1,0},{2,1},{3,2},{4,7},{5,4},{6,5},{7,6},{8,11},{9,8},{10,9... | collective-permute-start | bytes 589832 | tf_op jit(solution)/shard_map/ppermute | solution.py:21
  (34 other events, 352.2 us)
